TPU v7x, 32 devices: a whole 2x2x4 slice. The times are simulated.
32 devices in a mesh: ctx: 16 (over z, y, core), tp: 2 (over x).
Axes of the slice: x: 2, y: 2, z: 4, core: 2. Of those that a mesh axis runs over, the one named last changes fastest.
Arguments:
- queries: bfloat16 [4096, 4096], P('ctx', 'tp'), may hold values from -5 to 5
- key_head_array: bfloat16 [4096, 1024], P('ctx', 'tp'), may hold values from -8 to 8
- value_head_array: bfloat16 [4096, 1024], P('ctx', 'tp'), may hold values from -6 to 6
- ssm_input: bfloat16 [4096, 4096], P('ctx', 'tp'), may hold values from -6 to 6
- ssm_gate: bfloat16 [4096, 4096], P('ctx', 'tp'), may hold values from -30 to 30
- ssm_write: bfloat16 [4096, 1024], P('ctx', 'tp'), may hold values from -2.5 to 2.5
- ssm_read: bfloat16 [4096, 1024], P('ctx', 'tp'), may hold values from -2.5 to 2.5
- step_size: float32 [64, 4096], P('tp', 'ctx'), may hold values from 0.005 to 0.1
- log_decay: float32 [64, 4096], P('tp', 'ctx'), may hold values from -1 to 0
- skip_gain: float32 [64], P('tp'), may hold values from 0.5 to 2
- norm_gain: float32 [4096], P('tp'), may hold values from 0.1 to 1.9
- out_weight: bfloat16 [4096, 2048], P('tp'), may hold values from -2 to 2
Outputs:
- attn_mixed: float32 [4096, 2048], P('ctx', 'tp')
- ssm_output: float32 [4096, 4096], P('ctx', 'tp')
All inputs are finite; a program needn't handle non-finite values.
Results may differ from a plain program's by a relative error of at most 0.0053.
Values may be sent and summed in bfloat16 or wider, within the bound.
No kernel may reach another device: no remote copies, remote signals or barrier semaphores. Data moves between devices by JAX's collectives and lax.ppermute only.
A program may use at most 128 MiB of HBM per device.

v0:
```python
import math
import jax
import jax.numpy as jnp
from jax import lax
from jax.sharding import PartitionSpec as P

HEAD_SIZE = 128
P_SIZE = 64
NS = 128
neg_big = -1e30


def prefix_2(x, axis, combine, identity, reverse):
    count, mine = (lax.axis_size(axis), lax.axis_index(axis))
    everything = jax.tree.map(lambda part: lax.all_gather(part, axis), x)
    start = jax.tree.map(
        lambda part, zero: jnp.broadcast_to(jnp.asarray(zero, part.dtype), part.shape), x, identity
    )

    def lap(k, before):
        at = count - 1 - k if reverse else k
        reached = at > mine if reverse else at < mine
        new = combine(before, jax.tree.map(lambda part: part[at], everything))
        return jax.tree.map(lambda a, b: jnp.where(reached, a, b), new, before)

    return lax.fori_loop(0, count, lap, start)


def broadcast(x, axis, root):
    mine = lax.axis_index(axis) == root
    return lax.psum(jnp.where(mine, x, jnp.zeros_like(x)), axis)


def online_update(running, query_blk, key_blk, value_blk, query_pos, key_pos, score_scale):
    top_old, total_old, acc_old = running
    scores = (
        jnp.einsum("qgrd,kgd->grqk", query_blk, key_blk, preferred_element_type=jnp.float32)
        * score_scale
    )
    allowed = key_pos[None, None, None, :] <= query_pos[None, None, :, None]
    top_block = jnp.max(jnp.where(allowed, scores, neg_big), axis=-1)
    top_new = jnp.maximum(top_old, top_block)
    weights = jnp.where(allowed, jnp.exp(scores - top_new[..., None]), 0.0)
    factor = jnp.exp(top_old - top_new)
    total_new = total_old * factor + jnp.sum(weights, axis=-1)
    acc_new = acc_old * factor[..., None] + jnp.einsum(
        "grqk,kgd->grqd",
        weights.astype(jnp.bfloat16),
        value_blk,
        preferred_element_type=jnp.float32,
    )
    return (top_new, total_new, acc_new)


def compose(earlier, later):
    return (earlier[0] * later[0], later[0][..., None, None] * earlier[1] + later[1])


def steps_for():
    return 4


def body(
    queries,
    key_head_array,
    value_head_array,
    ssm_input,
    ssm_gate,
    ssm_write,
    ssm_read,
    step_size,
    log_decay,
    skip_gain,
    norm_gain,
    out_weight,
):
    ctx_count = lax.axis_size("ctx")
    ctx_index = lax.axis_index("ctx")
    tok_dev = queries.shape[0]
    half = tok_dev // 2
    kv_dev = key_head_array.shape[1] // HEAD_SIZE
    heads_dev = queries.shape[1] // HEAD_SIZE
    group_repeat = heads_dev // kv_dev
    score_scale = 1.0 / math.sqrt(HEAD_SIZE)
    last_block = 2 * ctx_count - 1
    row_ids = jnp.arange(half, dtype=jnp.int32)
    early_qpos = ctx_index * half + row_ids
    late_qpos = (last_block - ctx_index) * half + row_ids
    query_early = queries[:half].reshape(half, kv_dev, group_repeat, HEAD_SIZE)
    query_late = queries[half:].reshape(half, kv_dev, group_repeat, HEAD_SIZE)

    def fresh_state():
        return (
            jnp.full((kv_dev, group_repeat, half), neg_big, jnp.float32),
            jnp.zeros((kv_dev, group_repeat, half), jnp.float32),
            jnp.zeros((kv_dev, group_repeat, half, HEAD_SIZE), jnp.float32),
        )

    key_piece = lax.all_gather(key_head_array, "ctx", axis=0, tiled=True)
    value_piece = lax.all_gather(value_head_array, "ctx", axis=0, tiled=True)
    shard_count = key_piece.shape[0] // tok_dev
    per_step = steps_for()
    turns = shard_count // per_step
    key_groups = key_piece.reshape(turns, per_step, 2, half, kv_dev, HEAD_SIZE)
    value_groups = value_piece.reshape(turns, per_step, 2, half, kv_dev, HEAD_SIZE)

    def one_turn(running_pair, inputs):
        key_grp, value_grp, turn_index = inputs
        base_shard = turn_index * per_step
        shard_ids = base_shard + jnp.arange(per_step, dtype=jnp.int32)
        early_kpos = (shard_ids[:, None] * half + row_ids[None, :]).reshape(-1)
        late_kpos = ((last_block - shard_ids)[:, None] * half + row_ids[None, :]).reshape(-1)
        early_keys = key_grp[:, 0].reshape(per_step * half, kv_dev, HEAD_SIZE)
        late_keys = key_grp[:, 1].reshape(per_step * half, kv_dev, HEAD_SIZE)
        early_vals = value_grp[:, 0].reshape(per_step * half, kv_dev, HEAD_SIZE)
        late_vals = value_grp[:, 1].reshape(per_step * half, kv_dev, HEAD_SIZE)
        run_early, run_late = running_pair
        run_early = lax.cond(
            base_shard <= ctx_index,
            lambda running_now: online_update(
                running_now,
                query_early,
                early_keys,
                early_vals,
                early_qpos,
                early_kpos,
                score_scale,
            ),
            lambda running_now: running_now,
            run_early,
        )
        run_late = online_update(
            run_late, query_late, early_keys, early_vals, late_qpos, early_kpos, score_scale
        )
        run_late = lax.cond(
            base_shard + per_step - 1 >= ctx_index,
            lambda running_now: online_update(
                running_now, query_late, late_keys, late_vals, late_qpos, late_kpos, score_scale
            ),
            lambda running_now: running_now,
            run_late,
        )
        return ((run_early, run_late), None)

    result_pair, unused_out = lax.scan(
        one_turn,
        (fresh_state(), fresh_state()),
        (key_groups, value_groups, jnp.arange(turns, dtype=jnp.int32)),
    )

    def finish(running):
        top_fin, total_fin, acc_fin = running
        heads_out = acc_fin / total_fin[..., None]
        return (
            jnp.transpose(heads_out, (2, 0, 1, 3))
            .reshape(half, heads_dev * HEAD_SIZE)
            .astype(jnp.bfloat16)
        )

    attn_heads = jnp.concatenate([finish(result_pair[0]), finish(result_pair[1])], axis=0)
    head_terms = jnp.dot(attn_heads, out_weight, preferred_element_type=jnp.float32)
    attn_mixed = lax.psum_scatter(head_terms, "tp", scatter_dimension=1, tiled=True)
    heads_ssm = step_size.shape[0]
    groups_dev = ssm_write.shape[1] // NS
    per_group = heads_ssm // groups_dev
    causal = row_ids[:, None] >= row_ids[None, :]
    skip_cols = skip_gain.reshape(groups_dev, per_group)
    gain_cols = norm_gain.reshape(groups_dev, per_group * P_SIZE)

    def block_parts(row_from):
        cum_decay = jnp.cumsum(log_decay[:, row_from : row_from + half], axis=1).reshape(
            groups_dev, per_group, half
        )
        step_blk = step_size[:, row_from : row_from + half].reshape(groups_dev, per_group, half)
        input_blk = ssm_input[row_from : row_from + half].reshape(
            half, groups_dev, per_group, P_SIZE
        )
        write_blk = ssm_write[row_from : row_from + half].reshape(half, groups_dev, NS)
        read_blk = ssm_read[row_from : row_from + half].reshape(half, groups_dev, NS)
        scaled = (
            input_blk.astype(jnp.float32) * jnp.transpose(step_blk, (2, 0, 1))[..., None]
        ).astype(jnp.bfloat16)
        inner_prod = jnp.einsum(
            "tgn,sgn->gts", read_blk, write_blk, preferred_element_type=jnp.float32
        )
        decay_gap = cum_decay[..., :, None] - cum_decay[..., None, :]
        mixing = jnp.where(
            causal, inner_prod[:, None] * jnp.exp(jnp.where(causal, decay_gap, 0.0)), 0.0
        ).astype(jnp.bfloat16)
        local_out = jnp.einsum(
            "gjts,sgjp->tgjp", mixing, scaled, preferred_element_type=jnp.float32
        )
        tail_decay = jnp.exp(cum_decay[..., -1:] - cum_decay)
        written = (
            jnp.transpose(write_blk, (1, 0, 2)).astype(jnp.float32)[:, None] * tail_decay[..., None]
        ).astype(jnp.bfloat16)
        block_state = jnp.einsum(
            "sgjp,gjsn->gjpn", scaled, written, preferred_element_type=jnp.float32
        )
        block_decay = jnp.exp(cum_decay[..., -1])
        return ((block_decay, block_state), (local_out, cum_decay, read_blk, input_blk, row_from))

    def block_output(entering, pieces):
        local_out, cum_decay, read_blk, input_blk, row_from = pieces
        carried = jnp.einsum(
            "tgn,gjpn->tgjp",
            read_blk.astype(jnp.float32),
            entering,
            precision=lax.Precision.HIGHEST,
        )
        mixed_out = (
            local_out
            + carried * jnp.transpose(jnp.exp(cum_decay), (2, 0, 1))[..., None]
            + skip_cols[None, :, :, None] * input_blk.astype(jnp.float32)
        )
        gate_blk = ssm_gate[row_from : row_from + half].reshape(
            half, groups_dev, per_group * P_SIZE
        )
        gated = mixed_out.reshape(half, groups_dev, per_group * P_SIZE) * jax.nn.silu(
            gate_blk.astype(jnp.float32)
        )
        mean_square = jnp.mean(gated * gated, axis=-1, keepdims=True)
        normed = gated * lax.rsqrt(mean_square + 1e-05) * gain_cols[None]
        return normed.reshape(half, heads_ssm * P_SIZE)

    early_elem, early_rest = block_parts(0)
    late_elem, late_rest = block_parts(half)
    unit_decay = jnp.ones((groups_dev, per_group), jnp.float32)
    zero_state = jnp.zeros((groups_dev, per_group, P_SIZE, NS), jnp.float32)
    prefix = prefix_2(
        (early_elem[0], early_elem[1]), "ctx", compose, (unit_decay, zero_state), False
    )
    inclusive = compose(prefix, early_elem)
    total_state = broadcast(inclusive[1], "ctx", ctx_count - 1)
    suffix = prefix_2((late_elem[0], late_elem[1]), "ctx", compose, (unit_decay, zero_state), True)
    late_entering = suffix[0][..., None, None] * total_state + suffix[1]
    ssm_output = jnp.concatenate(
        [block_output(prefix[1], early_rest), block_output(late_entering, late_rest)], axis=0
    )
    return (attn_mixed, ssm_output)


def solution(mesh):
    placed = (
        P("ctx", "tp"),
        P("ctx", "tp"),
        P("ctx", "tp"),
        P("ctx", "tp"),
        P("ctx", "tp"),
        P("ctx", "tp"),
        P("ctx", "tp"),
        P("tp", "ctx"),
        P("tp", "ctx"),
        P("tp"),
        P("tp"),
        P("tp", None),
    )
    return jax.shard_map(
        body,
        mesh=mesh,
        in_specs=placed,
        out_specs=(P("ctx", "tp"), P("ctx", "tp")),
        check_vma=False,
    )
```

profile of v0, /device:TPU:0, one launch (start us, length us, event | category | flops | bytes accessed | tf_op | source)
XLA Modules:
  0.0 505.0 jit_solution(12839579409607009505)
XLA Ops:
  24.7 2.5 fusion.67
  42.0 24.4 %all-gather = f32[64,8,1]{1,2,0:T(1,128)} all-gather(f32[4,8,1]{1,2,0:T(1,128)} %bitcast.327), channel_id=2, replica_groups=mesh['ctx'=16,'tp'=2] {'ctx'}, dimensions={0}, use_global_device_ids=true | all-gather | bytes 2176 | tf_op jit(solution)/shard_map/all_gather | solution.py:15
  66.4 19.0 %all-gather.2 = f32[64,8,1]{1,2,0:T(1,128)} all-gather(f32[4,8,1]{1,2,0:T(1,128)} %bitcast.328), channel_id=4, replica_groups=mesh['ctx'=16,'tp'=2] {'ctx'}, dimensions={0}, use_global_device_ids=true | all-gather | bytes 2176 | tf_op jit(solution)/shard_map/all_gather | solution.py:15
  87.9 2.7 convolution_bitcast_fusion.2
  92.6 7.0 %reshape.295 = bf16[4,4,2,128,4,128]{5,4,3,2,1,0:T(4,128)(2,1)} reshape(bf16[4096,512]{1,0:T(8,128)(2,1)} %all-gather.9.cloned.1.call-done) | data formatting | bytes 8388608 | tf_op jit(solution)/shard_map/reshape | solution.py:104
  99.5 15.5 %all-gather.11.cloned.1.call-done = bf16[4096,512]{1,0:T(8,128)(2,1)} async-done(((bf16[256,512]{1,0:T(8,128)(2,1)}), bf16[4096,512]{1,0:T(8,128)(2,1)}) %all-gather.11.cloned.1.call-update) | async-done | bytes 4194320 | tf_op jit(solution)/shard_map/all_gather | solution.py:100
  115.0 6.9 %reshape.296 = bf16[4,4,2,128,4,128]{5,4,3,2,1,0:T(4,128)(2,1)} reshape(bf16[4096,512]{1,0:T(8,128)(2,1)} %all-gather.11.cloned.1.call-done) | data formatting | bytes 8388608 | tf_op jit(solution)/shard_map/reshape | solution.py:105
  124.1 57.9 %while.58 = (s32[]{:T(128)}, f32[4,4,128]{2,1,0:T(4,128)S(1)}, f32[4,4,128]{2,1,0:T(4,128)S(1)}, f32[4,4,128,128]{3,2,1,0:T(8,128)}, f32[4,4,128]{2,1,0:T(4,128)...) while((s32[]{:T(128)}, f32[4,4,128]{2,1,0:T(4,128)S(1)}, ...), condition=%wide.region_11.12_spmd.clone.clone, body=%wide.region_0.11_spmd.clone.clone.sunk | while | flops 1646999296 | bytes 91899224 | solution.py:145
  132.8 4.5 conditional.9
  137.3 5.6 %conditional.8 = ((f32[4,4,128]{2,1,0:T(4,128)S(1)}, f32[4,4,128]{2,1,0:T(4,128)S(1)}, f32[4,4,128,128]{3,2,1,0:T(8,128)})) conditional(s32[]{:T(128)} %convert_element_type.198, (f32[4,4,128]{2,1,0:T(4,128)S(1)}, f32[4,4,128]{2,1,0:T(4,128)S(1)}, f32[4,4,128,128]{3,2,1,0:T(8,128)}) %tuple.174, (s32[4]{0:T(128)S(1)}, s32[128]{0:T(128)S(1)}, ...), branch_computations={%region_1.1_spmd, %region_2.4_spmd} | conditional | flops 548999808 | bytes 27138184 | solution.py:118
  151.4 4.5 conditional.9
  164.4 4.5 conditional.9
  177.4 4.5 conditional.9
  186.4 56.2 %all-gather.13.cloned.1.call-done = f32[64,8,64,128]{3,2,1,0:T(8,128)} async-done(((f32[4,8,64,128]{3,2,1,0:T(8,128)}), f32[64,8,64,128]{3,2,1,0:T(8,128)}) %all-gather.13.cloned.1.call-update) | async-done | bytes 16777232 | tf_op jit(solution)/shard_map/all_gather | solution.py:15
  242.6 34.7 %while.59 = (s32[]{:T(128)}, f32[4,8,64,128]{3,2,1,0:T(8,128)S(1)}, s32[]{:T(128)}, f32[16,4,8]{2,1,0:T(4,128)}, f32[16,4,8,64,128]{4,3,2,1,0:T(8,128)}, /*index=5*/s32[]{:T(128)}, s32[]{:T(128)}) while((s32[]{:T(128)}, f32[4,8,64,128]{3,2,1,0:T(8,128)S(1)}, s32[]{:T(128)}, f32[16,4,8]{2,1,0:T(4,128)}, ...), condition=%wide.region_15.16_spmd.clone, body=%wide.region_14.15_spmd.clone.sunk | while | flops 1048580 | bytes 3146217 | solution.py:26
  278.7 7.2 %fusion.68 = f32[256,2048]{1,0:T(8,128)} fusion(bf16[2048,2048]{1,0:T(8,128)(2,1)} %param.33, bf16[128,2048]{0,1:T(8,128)(2,1)S(1)} %bitcast.292, bf16[128,2048]{0,1:T(8,128)(2,1)S(1)} %bitcast.293), kind=kOutput, calls=%fused_computation.96 | convolution fusion | flops 2149580800 | bytes 11534336 | tf_op jit(solution)/shard_map/dot_general | solution.py:161
  285.9 83.8 %all-gather.15.cloned.1.call-done = f32[64,8,64,128]{3,2,1,0:T(8,128)} async-done(((f32[4,8,64,128]{3,2,1,0:T(8,128)}), f32[64,8,64,128]{3,2,1,0:T(8,128)}) %all-gather.15.cloned.1.call-update) | async-done | bytes 16777232 | tf_op jit(solution)/shard_map/all_gather | solution.py:15
  369.7 34.7 %while.60 = (s32[]{:T(128)}, f32[4,8]{1,0:T(4,128)S(1)}, f32[4,8,64,128]{3,2,1,0:T(8,128)S(1)}, s32[]{:T(128)}, f32[16,4,8]{2,1,0:T(4,128)}, /*index=5*/f32[16,4...) while((s32[]{:T(128)}, f32[4,8]{1,0:T(4,128)S(1)}, ...), condition=%wide.region_19.20_spmd.clone, body=%wide.region_18.19_spmd.clone.sunk | while | flops 1048680 | bytes 3146545 | solution.py:26
  404.5 3.5 multiply_reduce_fusion.1
  408.7 2.5 copy.128
  411.2 53.2 %all-reduce.2.cloned.1.call-done = f32[4,8,64,128]{3,2,1,0:T(8,128)} async-done(((f32[4,8,64,128]{3,2,1,0:T(8,128)}), f32[4,8,64,128]{3,2,1,0:T(8,128)}) %all-reduce.2.cloned.1.call-update) | async-done | bytes 1048592 | tf_op jit(solution)/shard_map/psum | solution.py:31
  464.4 3.9 multiply_reduce_fusion
  470.0 2.5 copy.140
  476.5 21.7 %reduce-scatter.2.cloned.1.call-done = f32[256,1024]{1,0:T(8,128)} async-done(((f32[256,2048]{1,0:T(8,128)}), f32[256,1024]{1,0:T(8,128)}) %reduce-scatter.2.cloned.1.call-update) | async-done | bytes 1048592 | tf_op jit(solution)/shard_map/reduce_scatter | solution.py:162
  (363 shorter events, 173.7 us)
Async XLA Ops:
  7.2 85.4 %all-gather.9.cloned.1.call-start = ((), (), s32[]{:S(2)}) async-start(), calls=%async_computation.1 | async-start | bytes 4456448 | tf_op jit(solution)/shard_map/all_gather | solution.py:99
  7.9 107.1 %all-gather.11.cloned.1.call-start = ((), (), s32[]{:S(2)}) async-start(), calls=%async_computation.2 | async-start | bytes 4456448 | tf_op jit(solution)/shard_map/all_gather | solution.py:100
  8.6 233.9 %all-gather.13.cloned.1.call-start = ((), (), s32[]{:S(2)}) async-start(), calls=%async_computation.5 | async-start | bytes 17825792 | tf_op jit(solution)/shard_map/all_gather | solution.py:15
  13.6 77.0 %copy-start.5 = (f32[128,2048]{0,1:T(8,128)}, f32[128,2048]{0,1:T(8,128)S(1)}, u32[]{:S(2)}) copy-start(f32[128,2048]{0,1:T(8,128)S(1)} %copy.119) | copy-start | bytes 3145732
  16.6 6.4 %copy-start.23 = (f32[128,4,8]{0,2,1:T(8,128)}, f32[128,4,8]{0,2,1:T(8,128)S(1)}, u32[]{:S(2)}) copy-start(f32[128,4,8]{0,2,1:T(8,128)S(1)} %get-tuple-element.990) | copy-start | bytes 49156
  19.6 350.1 %all-gather.15.cloned.1.call-start = ((), (), s32[]{:S(2)}) async-start(), calls=%async_computation.6 | async-start | bytes 17825792 | tf_op jit(solution)/shard_map/all_gather | solution.py:15
  23.0 6.7 %copy-start.7 = (f32[128,2048]{0,1:T(8,128)}, f32[128,2048]{0,1:T(8,128)S(1)}, u32[]{:S(2)}) copy-start(f32[128,2048]{0,1:T(8,128)S(1)} %copy.131) | copy-start | bytes 3145732
  23.0 5.5 %copy-start.26 = (f32[4,8,1]{1,0,2:T(4,128)S(1)}, f32[4,8,1]{1,0,2:T(4,128)}, u32[]{:S(2)}) copy-start(f32[4,8,1]{1,0,2:T(4,128)} %copy.171) | copy-start | bytes 388
  23.0 6.0 %copy-start.21 = (bf16[256,512]{1,0:T(8,128)(2,1)S(1)}, bf16[256,512]{1,0:T(8,128)(2,1)}, u32[]{:S(2)}) copy-start(bf16[256,512]{1,0:T(8,128)(2,1)} %param.28) | copy-start | bytes 786436
  27.3 437.2 %all-reduce.2.cloned.1.call-start = ((), (), s32[]{:S(2)}) async-start(), calls=%async_computation.4 | async-start | bytes 2097152 | tf_op jit(solution)/shard_map/psum | solution.py:31
  36.9 51.0 %copy-start.8 = (f32[128,2048]{0,1:T(8,128)S(1)}, f32[128,2048]{0,1:T(8,128)}, u32[]{:S(2)}) copy-start(f32[128,2048]{0,1:T(8,128)} %copy-done.7) | copy-start | bytes 3145732
  42.0 48.7 %copy-start.24 = (f32[128,4,8]{0,2,1:T(8,128)S(1)}, f32[128,4,8]{0,2,1:T(8,128)}, u32[]{:S(2)}) copy-start(f32[128,4,8]{0,2,1:T(8,128)} %copy-done.23) | copy-start | bytes 49156
  181.9 60.7 %copy-start = (f32[4,8,64,128]{3,2,1,0:T(8,128)S(1)}, f32[4,8,64,128]{3,2,1,0:T(8,128)}, u32[]{:S(2)}) copy-start(f32[4,8,64,128]{3,2,1,0:T(8,128)} %custom-call) | copy-start | bytes 3145732
  242.6 34.7 %copy-start.4 = (f32[4,8,64,128]{3,2,1,0:T(8,128)S(1)}, f32[4,8,64,128]{3,2,1,0:T(8,128)}, u32[]{:S(2)}) copy-start(f32[4,8,64,128]{3,2,1,0:T(8,128)} %fusion.66) | copy-start | bytes 3145732
  242.6 34.7 %copy-start.29 = (f32[4,8]{1,0:T(4,128)S(1)}, f32[4,8]{1,0:T(4,128)}, u32[]{:S(2)}) copy-start(f32[4,8]{1,0:T(4,128)} %bitcast_exponential_fusion) | copy-start | bytes 388
  278.5 219.7 %reduce-scatter.2.cloned.1.call-start = ((), (), s32[]{:S(2)}) async-start(), calls=%async_computation.3 | async-start | bytes 3145728 | tf_op jit(solution)/shard_map/reduce_scatter | solution.py:162
  278.7 91.0 %copy-start.1 = (f32[4,8,64,128]{3,2,1,0:T(8,128)S(1)}, f32[4,8,64,128]{3,2,1,0:T(8,128)}, u32[]{:S(2)}) copy-start(f32[4,8,64,128]{3,2,1,0:T(8,128)} %custom-call.2) | copy-start | bytes 3145732
  278.7 91.0 %copy-start.25 = (f32[4,8]{1,0:T(4,128)S(1)}, f32[4,8]{1,0:T(4,128)}, u32[]{:S(2)}) copy-start(f32[4,8]{1,0:T(4,128)} %custom-call.1) | copy-start | bytes 388
  369.7 34.8 %copy-start.6 = (f32[128,2048]{0,1:T(8,128)S(1)}, f32[128,2048]{0,1:T(8,128)}, u32[]{:S(2)}) copy-start(f32[128,2048]{0,1:T(8,128)} %copy-done.5) | copy-start | bytes 3145732
  369.7 34.8 %copy-start.20 = (bf16[128,512]{0,1:T(8,128)(2,1)S(1)}, bf16[128,512]{0,1:T(8,128)(2,1)}, u32[]{:S(2)}) copy-start(bf16[128,512]{0,1:T(8,128)(2,1)} %copy.166) | copy-start | bytes 393220
  369.7 34.8 %copy-start.27 = (f32[128,4,8]{0,2,1:T(8,128)S(1)}, f32[128,4,8]{0,2,1:T(8,128)}, u32[]{:S(2)}) copy-start(f32[128,4,8]{0,2,1:T(8,128)} %get-tuple-element.994) | copy-start | bytes 49156
  369.7 34.8 %copy-start.31 = (f32[4,8]{1,0:T(4,128)S(1)}, f32[4,8]{1,0:T(4,128)}, u32[]{:S(2)}) copy-start(f32[4,8]{1,0:T(4,128)} %mul.374) | copy-start | bytes 388
  408.0 56.5 %copy-start.9 = (f32[128,2048]{0,1:T(8,128)S(1)}, f32[128,2048]{0,1:T(8,128)}, u32[]{:S(2)}) copy-start(f32[128,2048]{0,1:T(8,128)} %copy-done.7) | copy-start | bytes 3145732
  408.0 56.5 %copy-start.28 = (f32[128,4,8]{0,2,1:T(8,128)S(1)}, f32[128,4,8]{0,2,1:T(8,128)}, u32[]{:S(2)}) copy-start(f32[128,4,8]{0,2,1:T(8,128)} %get-tuple-element.996) | copy-start | bytes 49156
  (29 other events, 48.8 us)
Sparse Core Ops, SparseCore 0:
  10.2 53.4 all-gather.8
  65.8 49.1 all-gather.10
  117.2 125.3 all-gather.12
  244.6 125.0 all-gather.14
  373.0 91.3 all-reduce.1
  467.1 31.0 reduce-scatter.1
where the time goes:
time: 509 us; the launch traced here: 505 us
  waiting for transfers between devices  232 us (46%)
  other arithmetic  82.9 us (16%)
  local copies, waits for them, and re-layouts  81.4 us (16%)
  matrix products  46.4 us (9%)
  blocking collectives  43.4 us (9%)
  between operations  14.5 us (3%)
    all_gather x2, waiting for transfers between devices, prefix_2(): everything = jax.tree.map(lambda part: lax.all_gather(part, axis), x)  140 us
    select_n x48, other arithmetic, lap(): return jax.tree.map(lambda a, b: jnp.where(reached, a, b), new, before)  57.9 us
    psum x1, waiting for transfers between devices, broadcast(): return lax.psum(jnp.where(mine, x, jnp.zeros_like(x)), axis)  53.2 us
    all_gather x2, blocking collectives, prefix_2(): everything = jax.tree.map(lambda part: lax.all_gather(part, axis), x)  43.4 us
    reduce_scatter x1, waiting for transfers between devices, body(): lax.psum_scatter(head_terms, 'tp', scatter_dimension=1, tiled=True)  21.7 us
    all_gather x1, waiting for transfers between devices, body(): value_piece = lax.all_gather(value_head_array, 'ctx', axis=0, tiled=True)  15.5 us
    dot_general x9, matrix products, online_update(): jnp.einsum('grqk,kgd->grqd', weights.astype(jnp.bfloat16), value_blk, pre...  13.6 us
    dynamic_slice x16, local copies, waits for them, and re-layouts, body(): lax.scan(one_turn, (fresh_state(), fresh_state()), (key_groups, value_gro...  13.4 us
  transfers between devices with their start and end apart: 6, of which 5 were waited for; matrix products, arithmetic and copies ran while one was open for 40% of the time, Pallas kernels for 0%

commit v1 on v0

--- a/solution.py
+++ b/solution.py
@@ -97,7 +97,19 @@
         )
 
     key_piece = lax.all_gather(key_head_array, "ctx", axis=0, tiled=True)
-    value_piece = lax.all_gather(value_head_array, "ctx", axis=0, tiled=True)
+    slots = jax.lax.axis_size("ctx")
+    pieces_in = [(kk, (kk + 1) % slots) for kk in range(slots)]
+    fields = [(kk, (kk - 1) % slots) for kk in range(slots)]
+    x_new, r1 = ([value_head_array], [value_head_array])
+    for _ in range(slots // 2):
+        x_new.append(jax.lax.ppermute(x_new[-1], "ctx", pieces_in))
+    for _ in range((slots - 1) // 2):
+        r1.append(jax.lax.ppermute(r1[-1], "ctx", fields))
+    value_piece = jnp.roll(
+        jnp.concatenate([*x_new[::-1], *r1[1:]], 0),
+        (jax.lax.axis_index("ctx") - slots // 2) * value_head_array.shape[0],
+        0,
+    )
     shard_count = key_piece.shape[0] // tok_dev
     per_step = steps_for()
     turns = shard_count // per_step

time: 509 us -> 484 us (0.951)
  waiting for transfers between devices: 232 us -> 164 us
  starting transfers between devices: 0.24 us -> 29 us
  local copies, waits for them, and re-layouts: 81.4 us -> 97.1 us
    all_gather x2, waiting for transfers between devices: 140 us -> 47.5 us  [prefix_2(): everything = jax.tree.map(lambda part: lax.all_gather(part, axis), x)]
    ppermute x0 -> x15, waiting for transfers between devices: none -> 41.2 us  [the longest x8 21.5 us: body(): x_new.append(jax.lax.ppermute(x_new[-1], 'ctx', pieces_in))]
    ppermute x0 -> x15, starting transfers between devices: none -> 28.8 us  [the longest x7 28.2 us: body(): r1.append(jax.lax.ppermute(r1[-1], 'ctx', fields))]
    all_gather x1 -> x0, waiting for transfers between devices: 15.5 us -> none  [body(): value_piece = lax.all_gather(value_head_array, 'ctx', axis=0, tiled=True)]
    unnamed x60 -> x129, local copies, waits for them, and re-layouts: 8.05 us -> 21 us
  transfers between devices with their start and end apart: 6 -> 20, of which waited for: 5 -> 13; matrix products, arithmetic and copies ran while one was open for 40% -> 46% of each run, Pallas kernels for 0% -> 0%
where the time goes in v1:
time: 484 us; the launch traced here: 480 us
  waiting for transfers between devices  164 us (34%)
  local copies, waits for them, and re-layouts  97.1 us (20%)
  other arithmetic  83.2 us (17%)
  matrix products  47.6 us (10%)
  blocking collectives  39.9 us (8%)
  starting transfers between devices  29 us (6%)
  between operations  14.5 us (3%)
    select_n x48, other arithmetic, lap(): return jax.tree.map(lambda a, b: jnp.where(reached, a, b), new, before)  58.1 us
    psum x1, waiting for transfers between devices, broadcast(): return lax.psum(jnp.where(mine, x, jnp.zeros_like(x)), axis)  53.2 us
    all_gather x2, waiting for transfers between devices, prefix_2(): everything = jax.tree.map(lambda part: lax.all_gather(part, axis), x)  47.5 us
    all_gather x2, blocking collectives, prefix_2(): everything = jax.tree.map(lambda part: lax.all_gather(part, axis), x)  39.9 us
    ppermute x7, starting transfers between devices, body(): r1.append(jax.lax.ppermute(r1[-1], 'ctx', fields))  28.2 us
    reduce_scatter x1, waiting for transfers between devices, body(): lax.psum_scatter(head_terms, 'tp', scatter_dimension=1, tiled=True)  21.7 us
    ppermute x8, waiting for transfers between devices, body(): x_new.append(jax.lax.ppermute(x_new[-1], 'ctx', pieces_in))  21.5 us
    unnamed x129, local copies, waits for them, and re-layouts  21 us
  transfers between devices with their start and end apart: 20, of which 13 were waited for; matrix products, arithmetic and copies ran while one was open for 46% of the time, Pallas kernels for 0%

profile of v1, /device:TPU:0, one launch (start us, length us, event | category | flops | bytes accessed | tf_op | source)
XLA Modules:
  0.0 479.8 jit_solution(8197840397143316918)
XLA Ops:
  25.6 12.1 %collective-permute-done = bf16[256,512]{1,0:T(8,128)(2,1)S(1)} collective-permute-done((bf16[256,512]{1,0:T(8,128)(2,1)S(1)}, bf16[256,512]{1,0:T(8,128)(2,1)S(1)}, u32[]{:S(2)}, u32[]{:S(2)}) %collective-permute-start) | collective-permute-done | bytes 262176 | tf_op jit(solution)/shard_map/ppermute | solution.py:105
  42.2 6.2 %collective-permute-done.1 = bf16[256,512]{1,0:T(8,128)(2,1)S(1)} collective-permute-done((bf16[256,512]{1,0:T(8,128)(2,1)S(1)}, bf16[256,512]{1,0:T(8,128)(2,1)S(1)}, u32[]{:S(2)}, u32[]{:S(2)}) %collective-permute-start.1) | collective-permute-done | bytes 262176 | tf_op jit(solution)/shard_map/ppermute | solution.py:105
  51.1 4.6 collective-permute-start.9
  71.4 4.7 collective-permute-start.11
  87.8 20.1 %all-gather = f32[64,8,1]{1,2,0:T(1,128)} all-gather(f32[4,8,1]{1,2,0:T(1,128)S(1)} %bitcast.327), channel_id=2, replica_groups=mesh['ctx'=16,'tp'=2] {'ctx'}, dimensions={0}, use_global_device_ids=true | all-gather | bytes 2176 | tf_op jit(solution)/shard_map/all_gather | solution.py:15
  108.0 19.7 %all-gather.2 = f32[64,8,1]{1,2,0:T(1,128)} all-gather(f32[4,8,1]{1,2,0:T(1,128)S(1)} %bitcast.328), channel_id=4, replica_groups=mesh['ctx'=16,'tp'=2] {'ctx'}, dimensions={0}, use_global_device_ids=true | all-gather | bytes 2176 | tf_op jit(solution)/shard_map/all_gather | solution.py:15
  132.4 6.2 %collective-permute-done.12 = bf16[256,512]{1,0:T(8,128)(2,1)S(1)} collective-permute-done((bf16[256,512]{1,0:T(8,128)(2,1)}, bf16[256,512]{1,0:T(8,128)(2,1)S(1)}, u32[]{:S(2)}, u32[]{:S(2)}) %collective-permute-start.12) | collective-permute-done | bytes 262176 | tf_op jit(solution)/shard_map/ppermute | solution.py:107
  138.6 4.5 collective-permute-start.13
  145.8 6.8 %collective-permute-done.13 = bf16[256,512]{1,0:T(8,128)(2,1)S(1)} collective-permute-done((bf16[256,512]{1,0:T(8,128)(2,1)S(1)}, bf16[256,512]{1,0:T(8,128)(2,1)S(1)}, u32[]{:S(2)}, u32[]{:S(2)}) %collective-permute-start.13) | collective-permute-done | bytes 262176 | tf_op jit(solution)/shard_map/ppermute | solution.py:107
  152.6 4.6 collective-permute-start.14
  175.2 7.0 %reshape.296 = bf16[4,4,2,128,4,128]{5,4,3,2,1,0:T(4,128)(2,1)} reshape(bf16[4096,512]{1,0:T(8,128)(2,1)} %constant_dynamic-slice_fusion.2) | data formatting | bytes 8388608 | tf_op jit(solution)/shard_map/reshape | solution.py:117
  182.2 6.9 %reshape.295 = bf16[4,4,2,128,4,128]{5,4,3,2,1,0:T(4,128)(2,1)} reshape(bf16[4096,512]{1,0:T(8,128)(2,1)} %all-gather.8.cloned.1.call-done) | data formatting | bytes 8388608 | tf_op jit(solution)/shard_map/reshape | solution.py:116
  191.3 57.9 %while.58 = (s32[]{:T(128)}, f32[4,4,128]{2,1,0:T(4,128)S(1)}, f32[4,4,128]{2,1,0:T(4,128)S(1)}, f32[4,4,128,128]{3,2,1,0:T(8,128)}, f32[4,4,128]{2,1,0:T(4,128)...) while((s32[]{:T(128)}, f32[4,4,128]{2,1,0:T(4,128)S(1)}, ...), condition=%wide.region_11.12_spmd.clone.clone, body=%wide.region_0.11_spmd.clone.clone.sunk | while | flops 1646999296 | bytes 91899224 | solution.py:157
  199.8 4.5 conditional.9
  204.3 5.6 %conditional.8 = ((f32[4,4,128]{2,1,0:T(4,128)S(1)}, f32[4,4,128]{2,1,0:T(4,128)S(1)}, f32[4,4,128,128]{3,2,1,0:T(8,128)})) conditional(s32[]{:T(128)} %convert_element_type.198, (f32[4,4,128]{2,1,0:T(4,128)S(1)}, f32[4,4,128]{2,1,0:T(4,128)S(1)}, f32[4,4,128,128]{3,2,1,0:T(8,128)}) %tuple.174, (s32[4]{0:T(128)S(1)}, s32[128]{0:T(128)S(1)}, ...), branch_computations={%region_1.1_spmd, %region_2.4_spmd} | conditional | flops 548999808 | bytes 27138184 | solution.py:130
  218.4 4.5 conditional.9
  231.7 4.5 conditional.9
  244.7 4.5 conditional.9
  253.7 34.9 %while.59 = (s32[]{:T(128)}, f32[4,8,64,128]{3,2,1,0:T(8,128)S(1)}, s32[]{:T(128)}, f32[16,4,8]{2,1,0:T(4,128)}, f32[16,4,8,64,128]{4,3,2,1,0:T(8,128)}, /*index=5*/s32[]{:T(128)}, s32[]{:T(128)}) while((s32[]{:T(128)}, f32[4,8,64,128]{3,2,1,0:T(8,128)S(1)}, s32[]{:T(128)}, f32[16,4,8]{2,1,0:T(4,128)}, ...), condition=%wide.region_15.16_spmd.clone, body=%wide.region_14.15_spmd.clone.sunk | while | flops 1048580 | bytes 3146217 | solution.py:26
  290.0 7.1 %fusion.68 = f32[256,2048]{1,0:T(8,128)} fusion(bf16[2048,2048]{1,0:T(8,128)(2,1)} %param.33, bf16[128,2048]{0,1:T(8,128)(2,1)S(1)} %bitcast.292, bf16[128,2048]{0,1:T(8,128)(2,1)S(1)} %bitcast.293), kind=kOutput, calls=%fused_computation.96 | convolution fusion | flops 2149580800 | bytes 11534336 | tf_op jit(solution)/shard_map/dot_general | solution.py:173
  297.1 47.5 %all-gather.12.cloned.1.call-done = f32[64,8,64,128]{3,2,1,0:T(8,128)} async-done(((f32[4,8,64,128]{3,2,1,0:T(8,128)}), f32[64,8,64,128]{3,2,1,0:T(8,128)}) %all-gather.12.cloned.1.call-update) | async-done | bytes 16777232 | tf_op jit(solution)/shard_map/all_gather | solution.py:15
  344.7 34.9 %while.60 = (s32[]{:T(128)}, f32[4,8]{1,0:T(4,128)S(1)}, f32[4,8,64,128]{3,2,1,0:T(8,128)S(1)}, s32[]{:T(128)}, f32[16,4,8]{2,1,0:T(4,128)}, /*index=5*/f32[16,4...) while((s32[]{:T(128)}, f32[4,8]{1,0:T(4,128)S(1)}, ...), condition=%wide.region_19.20_spmd.clone, body=%wide.region_18.19_spmd.clone.sunk | while | flops 1048680 | bytes 3146545 | solution.py:26
  386.4 53.2 %all-reduce.2.cloned.1.call-done = f32[4,8,64,128]{3,2,1,0:T(8,128)} async-done(((f32[4,8,64,128]{3,2,1,0:T(8,128)}), f32[4,8,64,128]{3,2,1,0:T(8,128)}) %all-reduce.2.cloned.1.call-update) | async-done | bytes 1048592 | tf_op jit(solution)/shard_map/psum | solution.py:31
  451.6 21.7 %reduce-scatter.2.cloned.1.call-done = f32[256,1024]{1,0:T(8,128)} async-done(((f32[256,2048]{1,0:T(8,128)}), f32[256,1024]{1,0:T(8,128)}) %reduce-scatter.2.cloned.1.call-update) | async-done | bytes 1048592 | tf_op jit(solution)/shard_map/reduce_scatter | solution.py:174
  (461 shorter events, 228.1 us)
Async XLA Ops:
  7.2 175.0 %all-gather.8.cloned.1.call-start = ((), (), s32[]{:S(2)}) async-start(), calls=%async_computation.1 | async-start | bytes 4456448 | tf_op jit(solution)/shard_map/all_gather | solution.py:99
  7.9 245.7 %all-gather.10.cloned.1.call-start = ((), (), s32[]{:S(2)}) async-start(), calls=%async_computation.4 | async-start | bytes 17825792 | tf_op jit(solution)/shard_map/all_gather | solution.py:15
  16.5 328.2 %all-gather.12.cloned.1.call-start = ((), (), s32[]{:S(2)}) async-start(), calls=%async_computation.5 | async-start | bytes 17825792 | tf_op jit(solution)/shard_map/all_gather | solution.py:15
  25.1 414.4 %all-reduce.2.cloned.1.call-start = ((), (), s32[]{:S(2)}) async-start(), calls=%async_computation.3 | async-start | bytes 2097152 | tf_op jit(solution)/shard_map/psum | solution.py:31
  25.1 12.6 %collective-permute-start = (bf16[256,512]{1,0:T(8,128)(2,1)S(1)}, bf16[256,512]{1,0:T(8,128)(2,1)S(1)}, u32[]{:S(2)}, u32[]{:S(2)}) collective-permute-start(bf16[256,512]{1,0:T(8,128)(2,1)S(1)} %copy-done.20), channel_id=1, source_target_pairs={{0,2},{2,4},{4,6},{6,8},{8,10},{10,12},{12,14},{14,16},{16,18},{18... | collective-permute-start | bytes 786440 | tf_op jit(solution)/shard_map/ppermute | solution.py:105
  37.8 10.7 %collective-permute-start.1 = (bf16[256,512]{1,0:T(8,128)(2,1)S(1)}, bf16[256,512]{1,0:T(8,128)(2,1)S(1)}, u32[]{:S(2)}, u32[]{:S(2)}) collective-permute-start(bf16[256,512]{1,0:T(8,128)(2,1)S(1)} %collective-permute-done), channel_id=1, source_target_pairs={{0,2},{2,4},{4,6},{6,8},{8,10},{10,12},{12,14},{14,16},{16,18},{18... | collective-permute-start | bytes 786440 | tf_op jit(solution)/shard_map/ppermute | solution.py:105
  37.8 13.3 %collective-permute-start.8 = (bf16[256,512]{1,0:T(8,128)(2,1)S(1)}, bf16[256,512]{1,0:T(8,128)(2,1)S(1)}, u32[]{:S(2)}, u32[]{:S(2)}) collective-permute-start(bf16[256,512]{1,0:T(8,128)(2,1)S(1)} %copy-done.20), channel_id=1, source_target_pairs={{0,30},{2,0},{4,2},{6,4},{8,6},{10,8},{12,10},{14,12},{16,14},{18,... | collective-permute-start | bytes 786440 | tf_op jit(solution)/shard_map/ppermute | solution.py:107
  48.4 9.3 %collective-permute-start.2 = (bf16[256,512]{1,0:T(8,128)(2,1)S(1)}, bf16[256,512]{1,0:T(8,128)(2,1)S(1)}, u32[]{:S(2)}, u32[]{:S(2)}) collective-permute-start(bf16[256,512]{1,0:T(8,128)(2,1)S(1)} %collective-permute-done.1), channel_id=1, source_target_pairs={{0,2},{2,4},{4,6},{6,8},{8,10},{10,12},{12,14},{14,16},{16,18},{18... | collective-permute-start | bytes 786440 | tf_op jit(solution)/shard_map/ppermute | solution.py:105
  51.1 10.6 %collective-permute-start.9 = (bf16[256,512]{1,0:T(8,128)(2,1)S(1)}, bf16[256,512]{1,0:T(8,128)(2,1)}, u32[]{:S(2)}, u32[]{:S(2)}) collective-permute-start(bf16[256,512]{1,0:T(8,128)(2,1)S(1)} %collective-permute-done.8), channel_id=1, source_target_pairs={{0,30},{2,0},{4,2},{6,4},{8,6},{10,8},{12,10},{14,12},{16,14},{18,... | collective-permute-start | bytes 786440 | tf_op jit(solution)/shard_map/ppermute | solution.py:107
  57.7 8.8 %collective-permute-start.3 = (bf16[256,512]{1,0:T(8,128)(2,1)S(1)}, bf16[256,512]{1,0:T(8,128)(2,1)}, u32[]{:S(2)}, u32[]{:S(2)}) collective-permute-start(bf16[256,512]{1,0:T(8,128)(2,1)S(1)} %collective-permute-done.2), channel_id=1, source_target_pairs={{0,2},{2,4},{4,6},{6,8},{8,10},{10,12},{12,14},{14,16},{16,18},{18... | collective-permute-start | bytes 786440 | tf_op jit(solution)/shard_map/ppermute | solution.py:105
  61.6 9.8 %collective-permute-start.10 = (bf16[256,512]{1,0:T(8,128)(2,1)}, bf16[256,512]{1,0:T(8,128)(2,1)}, u32[]{:S(2)}, u32[]{:S(2)}) collective-permute-start(bf16[256,512]{1,0:T(8,128)(2,1)} %collective-permute-done.9), channel_id=1, source_target_pairs={{0,30},{2,0},{4,2},{6,4},{8,6},{10,8},{12,10},{14,12},{16,14},{18,... | collective-permute-start | bytes 786440 | tf_op jit(solution)/shard_map/ppermute | solution.py:107
  66.5 10.1 %collective-permute-start.4 = (bf16[256,512]{1,0:T(8,128)(2,1)}, bf16[256,512]{1,0:T(8,128)(2,1)}, u32[]{:S(2)}, u32[]{:S(2)}) collective-permute-start(bf16[256,512]{1,0:T(8,128)(2,1)} %collective-permute-done.3), channel_id=1, source_target_pairs={{0,2},{2,4},{4,6},{6,8},{8,10},{10,12},{12,14},{14,16},{16,18},{18... | collective-permute-start | bytes 786440 | tf_op jit(solution)/shard_map/ppermute | solution.py:105
  71.4 56.5 %collective-permute-start.11 = (bf16[256,512]{1,0:T(8,128)(2,1)}, bf16[256,512]{1,0:T(8,128)(2,1)}, u32[]{:S(2)}, u32[]{:S(2)}) collective-permute-start(bf16[256,512]{1,0:T(8,128)(2,1)} %collective-permute-done.10), channel_id=1, source_target_pairs={{0,30},{2,0},{4,2},{6,4},{8,6},{10,8},{12,10},{14,12},{16,14},{18,... | collective-permute-start | bytes 786440 | tf_op jit(solution)/shard_map/ppermute | solution.py:107
  76.6 52.3 %collective-permute-start.5 = (bf16[256,512]{1,0:T(8,128)(2,1)}, bf16[256,512]{1,0:T(8,128)(2,1)}, u32[]{:S(2)}, u32[]{:S(2)}) collective-permute-start(bf16[256,512]{1,0:T(8,128)(2,1)} %collective-permute-done.4), channel_id=1, source_target_pairs={{0,2},{2,4},{4,6},{6,8},{8,10},{10,12},{12,14},{14,16},{16,18},{18... | collective-permute-start | bytes 786440 | tf_op jit(solution)/shard_map/ppermute | solution.py:105
  84.0 59.1 %copy-start.6 = (f32[128,2048]{0,1:T(8,128)S(1)}, f32[128,2048]{0,1:T(8,128)}, u32[]{:S(2)}) copy-start(f32[128,2048]{0,1:T(8,128)} %copy-done.5) | copy-start | bytes 3145732
  127.9 10.7 %collective-permute-start.12 = (bf16[256,512]{1,0:T(8,128)(2,1)}, bf16[256,512]{1,0:T(8,128)(2,1)S(1)}, u32[]{:S(2)}, u32[]{:S(2)}) collective-permute-start(bf16[256,512]{1,0:T(8,128)(2,1)} %collective-permute-done.11), channel_id=1, source_target_pairs={{0,30},{2,0},{4,2},{6,4},{8,6},{10,8},{12,10},{14,12},{16,14},{18,... | collective-permute-start | bytes 786440 | tf_op jit(solution)/shard_map/ppermute | solution.py:107
  128.9 14.2 %collective-permute-start.6 = (bf16[256,512]{1,0:T(8,128)(2,1)}, bf16[256,512]{1,0:T(8,128)(2,1)S(1)}, u32[]{:S(2)}, u32[]{:S(2)}) collective-permute-start(bf16[256,512]{1,0:T(8,128)(2,1)} %collective-permute-done.5), channel_id=1, source_target_pairs={{0,2},{2,4},{4,6},{6,8},{8,10},{10,12},{12,14},{14,16},{16,18},{18... | collective-permute-start | bytes 786440 | tf_op jit(solution)/shard_map/ppermute | solution.py:105
  138.6 14.0 %collective-permute-start.13 = (bf16[256,512]{1,0:T(8,128)(2,1)S(1)}, bf16[256,512]{1,0:T(8,128)(2,1)S(1)}, u32[]{:S(2)}, u32[]{:S(2)}) collective-permute-start(bf16[256,512]{1,0:T(8,128)(2,1)S(1)} %collective-permute-done.12), channel_id=1, source_target_pairs={{0,30},{2,0},{4,2},{6,4},{8,6},{10,8},{12,10},{14,12},{16,14},{18,... | collective-permute-start | bytes 786440 | tf_op jit(solution)/shard_map/ppermute | solution.py:107
  143.1 14.1 %collective-permute-start.7 = (bf16[256,512]{1,0:T(8,128)(2,1)S(1)}, bf16[256,512]{1,0:T(8,128)(2,1)S(1)}, u32[]{:S(2)}, u32[]{:S(2)}) collective-permute-start(bf16[256,512]{1,0:T(8,128)(2,1)S(1)} %collective-permute-done.6), channel_id=1, source_target_pairs={{0,2},{2,4},{4,6},{6,8},{8,10},{10,12},{12,14},{14,16},{16,18},{18... | collective-permute-start | bytes 786440 | tf_op jit(solution)/shard_map/ppermute | solution.py:105
  152.6 14.1 %collective-permute-start.14 = (bf16[256,512]{1,0:T(8,128)(2,1)S(1)}, bf16[256,512]{1,0:T(8,128)(2,1)S(1)}, u32[]{:S(2)}, u32[]{:S(2)}) collective-permute-start(bf16[256,512]{1,0:T(8,128)(2,1)S(1)} %collective-permute-done.13), channel_id=1, source_target_pairs={{0,30},{2,0},{4,2},{6,4},{8,6},{10,8},{12,10},{14,12},{16,14},{18,... | collective-permute-start | bytes 786440 | tf_op jit(solution)/shard_map/ppermute | solution.py:107
  289.8 183.4 %reduce-scatter.2.cloned.1.call-start = ((), (), s32[]{:S(2)}) async-start(), calls=%async_computation.2 | async-start | bytes 3145728 | tf_op jit(solution)/shard_map/reduce_scatter | solution.py:174
  383.1 56.4 %copy-start.9 = (f32[128,2048]{0,1:T(8,128)S(1)}, f32[128,2048]{0,1:T(8,128)}, u32[]{:S(2)}) copy-start(f32[128,2048]{0,1:T(8,128)} %copy-done.8) | copy-start | bytes 3145732
  383.1 56.4 %copy-start.30 = (bf16[128,512]{0,1:T(8,128)(2,1)S(1)}, bf16[128,512]{0,1:T(8,128)(2,1)}, u32[]{:S(2)}) copy-start(bf16[128,512]{0,1:T(8,128)(2,1)} %copy-done.29) | copy-start | bytes 393220
  383.1 56.4 %copy-start.44 = (f32[128,4,8]{0,2,1:T(8,128)S(1)}, f32[128,4,8]{0,2,1:T(8,128)}, u32[]{:S(2)}) copy-start(f32[128,4,8]{0,2,1:T(8,128)} %get-tuple-element.996) | copy-start | bytes 49156
  (62 other events, 921.2 us)
Sparse Core Ops, SparseCore 0:
  10.2 64.1 all-gather.7
  76.5 138.4 all-gather.9
  217.2 127.4 all-gather.11
  348.0 91.4 all-reduce.1
  442.2 31.0 reduce-scatter.1
